TPU v7x, 512 devices: a whole 4x4x16 slice. The times are simulated.
512 devices in a mesh: pipe: 32 (over y_hi, z), expert: 16 (over x, y_lo, core).
Axes of the slice: x: 4, y: 4 (y_hi: 2, y_lo: 2; y = y_hi * 2 + y_lo), z: 16, core: 2. Of those that a mesh axis runs over, the one named last changes fastest.
Arguments:
- grad_out: bfloat16 [2, 32768, 3584], P(None, ('pipe', 'expert')), may hold values from -6 to 6
- route_slot: int32 [2, 32768], P(None, ('pipe', 'expert')), may hold values from -1 to 39, as said below
- gate_weight: float32 [2, 32768], P(None, ('pipe', 'expert')), may hold values from 0.3 to 1.5
- stored_pre: bfloat16 [32, 16, 40, 2, 2048], P('pipe', None, None, None, 'expert'), may hold values from -6 to 6
- w_in: bfloat16 [32, 2048, 2, 3584], P('pipe', 'expert'), may hold values from -0.09375 to 0.09375
- w_out: bfloat16 [32, 2048, 3584], P('pipe', 'expert'), may hold values from -0.1875 to 0.1875
Outputs:
- received: bfloat16 [2, 32768, 3584], P(None, ('pipe', 'expert'))
Inputs may be any that keep to these rules, and one draw needn't show every extreme that they name: `route_slot`: in each device's block of 64 tokens of one direction exactly 40 tokens carry a slot, each slot 0 to 39 taken once; the other tokens carry -1.
All inputs are finite; a program needn't handle non-finite values.
Results may differ from a plain program's by a relative error of at most 0.0054.
Values may be sent and summed in bfloat16 or wider, within the bound.
A program may use at most 64 MiB of HBM per device.

v0:
```python
import jax
import jax.numpy as jnp
from jax import lax
from jax.sharding import PartitionSpec as P


def from_behind(value, axis, steps):
    count = lax.axis_size(axis)
    first, last = (max(0, -steps), min(count, count - steps))
    return lax.ppermute(value, axis, [(source, source + steps) for source in range(first, last)])


def swiglu_back(hidden_grad, gate_pre, up_pre):
    gate_pre = gate_pre.astype(jnp.float32)
    up_pre = up_pre.astype(jnp.float32)
    squashed = jax.nn.sigmoid(gate_pre)
    gate_grad = hidden_grad * up_pre * squashed * (1.0 + gate_pre * (1.0 - squashed))
    up_grad = hidden_grad * gate_pre * squashed
    return jnp.stack([gate_grad, up_grad], axis=-1)


def pack_rows(gradient, slot_rows, gate_rows, capacity):
    scaled = (gate_rows[:, None] * gradient.astype(jnp.float32)).astype(jnp.bfloat16)
    onehot = (slot_rows[:, None] == jnp.arange(capacity, dtype=jnp.int32)[None, :]).astype(
        jnp.bfloat16
    )
    packed = lax.dot_general(
        onehot, scaled, (((0,), (0,)), ((), ())), preferred_element_type=jnp.float32
    )
    return packed.astype(jnp.bfloat16)


def expert_partial(arrived, stored_rows, weight_in, weight_out):
    row_count, capacity, features = arrived.shape
    flat_rows = arrived.reshape(row_count * capacity, features)
    hidden_grad = lax.dot_general(
        flat_rows, weight_out, (((1,), (1,)), ((), ())), preferred_element_type=jnp.float32
    )
    pre_act = stored_rows.reshape(row_count * capacity, 2, -1)
    pre_grad = swiglu_back(hidden_grad, pre_act[:, 0], pre_act[:, 1]).astype(jnp.bfloat16)
    partial_value = jnp.dot(
        pre_grad.reshape(row_count * capacity, -1),
        weight_in.reshape(-1, features),
        preferred_element_type=jnp.float32,
    )
    return partial_value.astype(jnp.bfloat16).reshape(row_count, capacity, features)


def on_device(grad_out, route_slot, gate_weight, stored_pre, w_in, w_out):
    experts = lax.axis_size("expert")
    half_count = experts // 2
    capacity = stored_pre.shape[2]
    weight_in = w_in[0]
    weight_out = w_out[0]
    stored_here = stored_pre[0]
    packed_rows = [
        pack_rows(grad_out[direction], route_slot[direction], gate_weight[direction], capacity)
        for direction in range(2)
    ]
    shape_one = (half_count,) + packed_rows[0].shape
    outgoing = jnp.concatenate(
        [
            jnp.broadcast_to(packed_rows[0][None], shape_one),
            jnp.broadcast_to(packed_rows[1][None], shape_one),
        ],
        axis=0,
    )
    arrived = lax.all_to_all(outgoing, "expert", split_axis=0, concat_axis=0, tiled=True)
    partial_value = expert_partial(arrived, stored_here, weight_in, weight_out)
    returned = lax.all_to_all(partial_value, "expert", split_axis=0, concat_axis=0, tiled=True)
    totals = [
        jnp.sum(returned[:half_count].astype(jnp.float32), axis=0),
        jnp.sum(returned[half_count:].astype(jnp.float32), axis=0),
    ]
    layer_grad = []
    for direction in range(2):
        slot_index = jnp.clip(route_slot[direction], 0, capacity - 1)
        picked = jnp.take(totals[direction], slot_index, axis=0)
        contrib = jnp.where(route_slot[direction][:, None] >= 0, picked, jnp.float32(0.0))
        layer_grad.append((grad_out[direction].astype(jnp.float32) + contrib).astype(jnp.bfloat16))
    downward = from_behind(layer_grad[0], "pipe", -1)
    upward = from_behind(layer_grad[1], "pipe", 1)
    return jnp.stack([downward, upward])


def solution(mesh):
    return jax.shard_map(
        on_device,
        mesh=mesh,
        in_specs=(
            P(None, ("pipe", "expert"), None),
            P(None, ("pipe", "expert")),
            P(None, ("pipe", "expert")),
            P("pipe", None, None, None, "expert"),
            P("pipe", "expert", None, None),
            P("pipe", "expert", None),
        ),
        out_specs=P(None, ("pipe", "expert"), None),
        check_vma=False,
    )
```

profile of v0, /device:TPU:25, one launch (start us, length us, event | category | flops | bytes accessed | tf_op | source)
XLA Modules:
  0.0 191.7 jit_solution(8903690902661417753)
XLA Ops:
  0.0 0.8 slice_bitcast_fusion.3
  0.8 0.8 slice_bitcast_fusion.2
  1.5 1.4 convolution_convert_fusion.2
  2.9 1.4 convolution_convert_fusion.1
  4.6 2.5 %pad_maximum_fusion = bf16[16,40,3584]{2,1,0:T(8,128)(2,1)} fusion(bf16[8,40,3584]{2,1,0:T(8,128)(2,1)S(1)} %broadcast_in_dim.43, bf16[8,40,3584]{2,1,0:T(8,128)(2,1)S(1)} %broadcast_in_dim.42), kind=kLoop, calls=%fused_computation.3 | loop fusion | flops 2293760 | bytes 9175040 | tf_op jit(solution)/shard_map/concatenate | solution.py:61
  7.1 6.2 %all-to-all-start = ((bf16[16,40,3584]{2,1,0:T(8,128)(2,1)}), bf16[16,40,3584]{2,1,0:T(8,128)(2,1)}, u32[]{:S(2)}, u32[]{:S(2)}) async-start(bf16[16,40,3584]{2,1,0:T(8,128)(2,1)} %pad_maximum_fusion), calls=%async_computation | async-start | bytes 9175040 | tf_op jit(solution)/shard_map/all_to_all | solution.py:68
  13.4 0.2 copy.12
  13.6 0.2 copy.13
  13.8 4.1 %reshape_squeeze.7 = bf16[256,3584]{1,0:T(8,128)(2,1)S(1)} reshape(bf16[1,128,2,3584]{3,2,1,0:T(2,128)(2,1)} %param.12) | data formatting | bytes 3670016 | tf_op jit(solution)/shard_map/reshape;squeeze | solution.py:43
  17.8 58.7 %all-to-all-done = bf16[16,40,3584]{2,1,0:T(8,128)(2,1)} async-done(((bf16[16,40,3584]{2,1,0:T(8,128)(2,1)}), bf16[16,40,3584]{2,1,0:T(8,128)(2,1)}, u32[]{:S(2)}, u32[]{:S(2)}) %all-to-all-start) | async-done | bytes 4587552 | tf_op jit(solution)/shard_map/all_to_all | solution.py:68
  76.5 3.8 %fusion.24 = (bf16[640,128,1]{0,1,2:T(8,128)(2,1)S(1)}, bf16[640,128,1]{0,1,2:T(8,128)(2,1)S(1)}) fusion(bf16[640,1,128]{0,2,1:T(8,128)(2,1)S(1)} %copy.13, bf16[640,1,128]{0,2,1:T(8,128)(2,1)S(1)} %copy.12, bf16[640,3584]{1,0:T(8,128)(2,1)} %bitcast.7, bf16[1,128,3584]{2,1,0:T(8,128)(2,1)S(1)} %copy-done), kind=kOutput, calls=%fused_computation.42 | convolution fusion | flops 588431360 | bytes 6160384 | tf_op jit(solution)/shard_map/dot_general | solution.py:36
  80.4 0.3 copy.11
  80.9 3.5 %convolution_convert_fusion = bf16[640,3584]{1,0:T(8,128)(2,1)} fusion(bf16[640,256]{0,1:T(8,128)(2,1)S(1)} %convert_element_type.78, bf16[256,3584]{1,0:T(8,128)(2,1)S(1)} %reshape_squeeze.7), kind=kOutput, calls=%fused_computation.2 | convolution fusion | flops 1176698880 | bytes 6750208 | tf_op jit(solution)/shard_map/dot_general | solution.py:41
  84.4 7.8 %all-to-all-start.1 = ((bf16[16,40,3584]{2,1,0:T(8,128)(2,1)}), bf16[16,40,3584]{2,1,0:T(8,128)(2,1)}, u32[]{:S(2)}, u32[]{:S(2)}) async-start(bf16[16,40,3584]{2,1,0:T(8,128)(2,1)} %bitcast.64), calls=%async_computation.1 | async-start | bytes 9175040 | tf_op jit(solution)/shard_map/all_to_all | solution.py:70
  92.2 63.1 %all-to-all-done.1 = bf16[16,40,3584]{2,1,0:T(8,128)(2,1)} async-done(((bf16[16,40,3584]{2,1,0:T(8,128)(2,1)}), bf16[16,40,3584]{2,1,0:T(8,128)(2,1)}, u32[]{:S(2)}, u32[]{:S(2)}) %all-to-all-start.1) | async-done | bytes 4587552 | tf_op jit(solution)/shard_map/all_to_all | solution.py:70
  155.3 3.1 %convert_reduce_fusion.1 = (f32[40,3584]{1,0:T(8,128)S(1)}, f32[40,3584]{1,0:T(8,128)S(1)}) fusion(bf16[16,40,3584]{2,1,0:T(8,128)(2,1)} %all-to-all-done.1), kind=kLoop, calls=%fused_computation.5 | loop fusion | flops 4300800 | bytes 5734400 | tf_op jit(solution)/shard_map/reduce_sum | solution.py:72
  158.4 0.9 gather_fusion.1
  159.3 0.9 gather_fusion
  160.2 1.6 fusion.1
  161.7 11.8 %collective-permute-start = (bf16[64,3584]{1,0:T(8,128)(2,1)S(1)}, bf16[64,3584]{1,0:T(8,128)(2,1)S(1)}, u32[]{:S(2)}, u32[]{:S(2)}) collective-permute-start(bf16[64,3584]{1,0:T(8,128)(2,1)S(1)} %get-tuple-element.12), channel_id=1, source_target_pairs={{16,0},{32,16},{48,32},{64,48},{80,64},{96,80},{112,96},{128,112},... | collective-permute-start | bytes 1376264 | tf_op jit(solution)/shard_map/ppermute | solution.py:10
  173.5 1.9 %collective-permute-start.1 = (bf16[64,3584]{1,0:T(8,128)(2,1)S(1)}, bf16[64,3584]{1,0:T(8,128)(2,1)S(1)}, u32[]{:S(2)}, u32[]{:S(2)}) collective-permute-start(bf16[64,3584]{1,0:T(8,128)(2,1)S(1)} %get-tuple-element.13), channel_id=1, source_target_pairs={{0,16},{16,32},{32,48},{48,64},{64,80},{80,96},{96,112},{112,128},... | collective-permute-start | bytes 1376264 | tf_op jit(solution)/shard_map/ppermute | solution.py:10
  175.5 7.8 %collective-permute-done = bf16[64,3584]{1,0:T(8,128)(2,1)S(1)} collective-permute-done((bf16[64,3584]{1,0:T(8,128)(2,1)S(1)}, bf16[64,3584]{1,0:T(8,128)(2,1)S(1)}, u32[]{:S(2)}, u32[]{:S(2)}) %collective-permute-start) | collective-permute-done | bytes 458784 | tf_op jit(solution)/shard_map/ppermute | solution.py:10
  183.2 7.4 %collective-permute-done.1 = bf16[64,3584]{1,0:T(8,128)(2,1)S(1)} collective-permute-done((bf16[64,3584]{1,0:T(8,128)(2,1)S(1)}, bf16[64,3584]{1,0:T(8,128)(2,1)S(1)}, u32[]{:S(2)}, u32[]{:S(2)}) %collective-permute-start.1) | collective-permute-done | bytes 458784 | tf_op jit(solution)/shard_map/ppermute | solution.py:10
  190.6 1.0 pad_maximum_fusion.1
  (14 shorter events, 0.6 us)
Async XLA Ops:
  0.0 76.5 %copy-start = (bf16[1,128,3584]{2,1,0:T(8,128)(2,1)S(1)}, bf16[1,128,3584]{2,1,0:T(8,128)(2,1)}, u32[]{:S(2)}) copy-start(bf16[1,128,3584]{2,1,0:T(8,128)(2,1)} %param.13) | copy-start | bytes 2752516
  7.1 6.2 %copy-start.1 = (bf16[1,16,40,2,128]{4,3,2,1,0:T(2,128)(2,1)S(1)}, bf16[1,16,40,2,128]{4,3,2,1,0:T(2,128)(2,1)}, u32[]{:S(2)}) copy-start(bf16[1,16,40,2,128]{4,3,2,1,0:T(2,128)(2,1)} %param.11) | copy-start | bytes 983044
  7.1 69.4 %all-to-all-start = ((bf16[16,40,3584]{2,1,0:T(8,128)(2,1)}), bf16[16,40,3584]{2,1,0:T(8,128)(2,1)}, u32[]{:S(2)}, u32[]{:S(2)}) async-start(bf16[16,40,3584]{2,1,0:T(8,128)(2,1)} %pad_maximum_fusion), calls=%async_computation | async-start | bytes 9175040 | tf_op jit(solution)/shard_map/all_to_all | solution.py:68
  84.4 7.8 %copy-start.2 = (s32[2,64]{1,0:T(2,128)S(1)}, s32[2,64]{1,0:T(2,128)}, u32[]{:S(2)}) copy-start(s32[2,64]{1,0:T(2,128)} %param.9) | copy-start | bytes 1540
  84.4 71.0 %all-to-all-start.1 = ((bf16[16,40,3584]{2,1,0:T(8,128)(2,1)}), bf16[16,40,3584]{2,1,0:T(8,128)(2,1)}, u32[]{:S(2)}, u32[]{:S(2)}) async-start(bf16[16,40,3584]{2,1,0:T(8,128)(2,1)} %bitcast.64), calls=%async_computation.1 | async-start | bytes 9175040 | tf_op jit(solution)/shard_map/all_to_all | solution.py:70
  161.7 21.5 %collective-permute-start = (bf16[64,3584]{1,0:T(8,128)(2,1)S(1)}, bf16[64,3584]{1,0:T(8,128)(2,1)S(1)}, u32[]{:S(2)}, u32[]{:S(2)}) collective-permute-start(bf16[64,3584]{1,0:T(8,128)(2,1)S(1)} %get-tuple-element.12), channel_id=1, source_target_pairs={{16,0},{32,16},{48,32},{64,48},{80,64},{96,80},{112,96},{128,112},... | collective-permute-start | bytes 1376264 | tf_op jit(solution)/shard_map/ppermute | solution.py:10
  173.5 17.1 %collective-permute-start.1 = (bf16[64,3584]{1,0:T(8,128)(2,1)S(1)}, bf16[64,3584]{1,0:T(8,128)(2,1)S(1)}, u32[]{:S(2)}, u32[]{:S(2)}) collective-permute-start(bf16[64,3584]{1,0:T(8,128)(2,1)S(1)} %get-tuple-element.13), channel_id=1, source_target_pairs={{0,16},{16,32},{32,48},{48,64},{64,80},{80,96},{96,112},{112,128},... | collective-permute-start | bytes 1376264 | tf_op jit(solution)/shard_map/ppermute | solution.py:10
where the time goes:
time: 195 us; the launch traced here: 192 us
  waiting for transfers between devices  137 us (70%)
  starting transfers between devices  27.7 us (14%)
  matrix products  10 us (5%)
  local copies, waits for them, and re-layouts  8.54 us (4%)
  other arithmetic  8.2 us (4%)
    all_to_all x1, waiting for transfers between devices, on_device(): lax.all_to_all(partial_value, 'expert', split_axis=0, concat_axis=0, tile...  63.1 us
    all_to_all x1, waiting for transfers between devices, on_device(): lax.all_to_all(outgoing, 'expert', split_axis=0, concat_axis=0, tiled=True)  58.7 us
    ppermute x2, waiting for transfers between devices, from_behind(): lax.ppermute(value, axis, [(source, source + steps) for source in range(f...  15.2 us
    ppermute x2, starting transfers between devices, from_behind(): lax.ppermute(value, axis, [(source, source + steps) for source in range(f...  13.7 us
    all_to_all x1, starting transfers between devices, on_device(): lax.all_to_all(partial_value, 'expert', split_axis=0, concat_axis=0, tile...  7.78 us
    all_to_all x1, starting transfers between devices, on_device(): lax.all_to_all(outgoing, 'expert', split_axis=0, concat_axis=0, tiled=True)  6.22 us
    another operation x1, local copies, waits for them, and re-layouts, expert_partial(): weight_in.reshape(-1, features)  4.06 us
  transfers between devices with their start and end apart: 4, of which 4 were waited for; matrix products, arithmetic and copies ran while one was open for 2% of the time, Pallas kernels for 0%

commit v1 on v0

v1 whole, which is shorter than its diff:
```python
import functools

import jax
import jax.numpy as jnp
from jax import lax
from jax.experimental import pallas as pl
from jax.experimental.pallas import tpu as pltpu
from jax.sharding import PartitionSpec as P

MESH = pl.DeviceIdType.MESH
F32, BF16 = jnp.float32, jnp.bfloat16
BLOCKS = [(c, f, s) for c in range(2) for f in range(2) for s in range(2)]


def number(block):
    return block[0] * 4 + block[1] * 2 + block[2]


def iota(shape, dim):
    return lax.broadcasted_iota(jnp.int32, shape, dim).astype(F32)


def kernel(
    n_pipe, capacity,
    grad_hbm, slot_ref, gate_ref, stored_hbm, w_in_hbm, w_out_hbm,
    out_hbm,
    grad_full, grad_chip, meta, w_out_chip, w_in_chip, stored_chip,
    raw, cross_block, x_block, hid_send, hid_recv, acc, ret_send, ret_sec,
    first_send, ret_first, cut_send, ret_cut, final, early, landed, out_buf,
    local_sem, send_sem, recv_sem,
):
    tokens, features = grad_full.shape[1:]
    half = features // 2
    p, e = lax.axis_index("pipe"), lax.axis_index("expert")
    core, y, x = e % 2, (e // 2) % 2, e // 4
    g = x // 2
    sibling = e + 1 - 2 * core
    x_next = e + 4 - 8 * (x % 2)
    y_next = e + 2 - 4 * y
    cut = e + 4 * (3 - 2 * x)
    first = x_next + core * (y_next - x_next)
    second = y_next + core * (x_next - y_next)
    base = e - core
    z_to = [p - 1 + 2 * g, p + 1 - 2 * g]
    z_from = [z_to[1], z_to[0]]

    def valid(rank):
        return jnp.logical_and(rank >= 0, rank < n_pipe)

    counter = [0]

    def take():
        counter[0] += 1
        return counter[0] - 1

    def remote(src, dst, device, index=None):
        index = take() if index is None else index
        return pltpu.make_async_remote_copy(
            src_ref=src, dst_ref=dst, send_sem=send_sem.at[index], recv_sem=recv_sem.at[index],
            device_id=device, device_id_type=MESH,
        )

    barrier = pltpu.get_barrier_semaphore()
    for other in (sibling, first, second, cut):
        pl.semaphore_signal(barrier, inc=1, device_id=(p, other), device_id_type=MESH)
    for rank in z_to:
        @pl.when(valid(rank))
        def _():
            for k in range(2):
                pl.semaphore_signal(barrier, inc=1, device_id=(rank, base + k), device_id_type=MESH)

    mine = pl.multiple_of(core * half, 128)
    theirs = pl.multiple_of((1 - core) * half, 128)

    def local(src, dst, index):
        return pltpu.make_async_copy(src, dst, local_sem.at[index])

    load_full = local(grad_hbm, grad_full, 0)
    load_half = local(grad_hbm.at[:, :, pl.ds(mine, half)], grad_chip.at[core], 1)
    load_out = local(w_out_hbm.at[:, pl.ds(mine, half)], w_out_chip.at[core], 2)
    load_in = local(w_in_hbm.at[:, :, pl.ds(mine, half)], w_in_chip.at[core], 3)
    load_stored = local(stored_hbm, stored_chip.at[core], 4)
    load_half.start()
    load_full.start()

    slot = slot_ref[...].astype(F32)
    gate = gate_ref[...]
    meta[0] = jnp.zeros_like(meta[0])
    meta[0, 0:2, 0:tokens] = slot
    meta[0, 0:2, tokens:2 * tokens] = slot
    meta[0, 2:4, 0:tokens] = gate
    meta[0, 2:4, tokens:2 * tokens] = gate

    pl.semaphore_wait(barrier, 4 + 2 * sum(valid(rank).astype(jnp.int32) for rank in z_to))

    pending = []

    def go(copy):
        copy.start()
        pending.append(copy)
        return copy

    got_meta = go(remote(meta.at[0], meta.at[1], (p, sibling)))
    got_grad = go(remote(
        grad_hbm.at[:, :, pl.ds(theirs, half)], grad_chip.at[core], (p, sibling)))
    load_out.start()
    load_stored.start()
    load_in.start()
    got_out = go(remote(w_out_hbm.at[:, pl.ds(theirs, half)], w_out_chip.at[core], (p, sibling)))
    got_stored = go(remote(stored_hbm, stored_chip.at[core], (p, sibling)))
    got_in = go(remote(w_in_hbm.at[:, :, pl.ds(theirs, half)], w_in_chip.at[core], (p, sibling)))

    load_half.wait()
    got_meta.wait_recv()
    got_grad.wait_recv()

    rows = 2 * capacity
    lane = lax.broadcasted_iota(jnp.int32, (1, 2 * tokens), 1)

    def pack(direction):
        own_slot = meta[0, pl.ds(direction, 1), :]
        sib_slot = meta[1, pl.ds(direction, 1), :]
        own_gate = meta[0, pl.ds(direction + 2, 1), :]
        sib_gate = meta[1, pl.ds(direction + 2, 1), :]
        is_own = (lane // tokens) == core
        chip_slot = jnp.where(is_own, own_slot, sib_slot)
        chip_gate = jnp.where(is_own, own_gate, sib_gate)
        chip_slot = jnp.where(
            jnp.logical_and(lane >= tokens, chip_slot >= 0), chip_slot + capacity, chip_slot)
        onehot = jnp.where(iota((rows, 2 * tokens), 0) == chip_slot, 1.0, 0.0)
        slot_gate = jnp.sum(onehot * chip_gate, axis=1, keepdims=True)
        both = jnp.concatenate([grad_chip[0, direction], grad_chip[1, direction]], axis=0)
        picked = jnp.dot(onehot.astype(BF16), both, preferred_element_type=F32)
        return picked.astype(BF16), (slot_gate * picked).astype(BF16)

    raw[1], cross_block[...] = pack(1 - g)
    got_x = {}
    got_x[1, 0, 0] = go(remote(cross_block, x_block.at[number((1, 0, 0))], (p, cut)))
    raw[0], x_block[0] = pack(g)

    def forward(block, along):
        c, f, s = block
        target = (c, 1, s) if along == "first" else (c, f, 1)
        device = first if along == "first" else second
        got_x[target] = go(remote(
            x_block.at[number(block)], x_block.at[number(target)], (p, device)))

    forward((0, 0, 0), "first")
    forward((0, 0, 0), "second")

    def unrouted(slot_row):
        free = jnp.where(slot_row < 0, 1.0, 0.0)
        before = jnp.where(
            iota((tokens, tokens), 0) < iota((tokens, tokens), 1), 1.0, 0.0).astype(BF16)
        wide = jnp.broadcast_to(free, (8, tokens)).astype(BF16)
        rank = jnp.dot(wide, before, preferred_element_type=F32)[0:1]
        return jnp.where(slot_row < 0, rank, -1.0)

    spare = early.shape[2]
    load_full.wait()
    z_early = []
    z_meta = []
    for w, direction in enumerate((g, 1 - g)):
        rank = unrouted(meta[0, pl.ds(direction, 1), 0:tokens])
        chosen = jnp.where(iota((spare, tokens), 0) == rank, 1.0, 0.0).astype(BF16)
        values = jnp.dot(chosen, grad_full[direction], preferred_element_type=F32).astype(BF16)
        early[w, 0] = values[:, :half]
        early[w, 1] = values[:, half:]
        z_meta.append(remote(meta.at[0], meta.at[2 + w], (z_to[w], e)))
        z_early.append(remote(
            early.at[w], landed.at[w, :, pl.ds(landed.shape[2] - spare, spare)], (z_to[w], e)))

        @pl.when(valid(z_to[w]))
        def _():
            z_meta[w].start()
            z_early[w].start()

    load_out.wait()
    got_out.wait_recv()
    hid_base = counter[0]
    counter[0] += len(BLOCKS)

    def swap(i, there):
        return pltpu.make_async_remote_copy(
            src_ref=hid_send.at[i], dst_ref=hid_recv.at[there],
            send_sem=send_sem.at[hid_base + i], recv_sem=recv_sem.at[hid_base + there],
            device_id=(p, sibling), device_id_type=MESH)

    def hidden(block):
        i = number(block)
        w_out = w_out_chip[...].reshape(-1, half)
        hid_send[i] = lax.dot_general(
            x_block[i], w_out, (((1,), (1,)), ((), ())), preferred_element_type=F32)
        there = number((block[0], block[2], block[1]))
        pending.append(swap(i, there))
        pending[-1].start()

    def finish(block):
        i = number(block)
        c, f, s = block
        dx = f + core * (s - f)
        dy = s + core * (f - s)
        at_x = (x // 2) * 2 + (x % 2 + dx) % 2
        at_x = at_x + c * (3 - 2 * at_x)
        chip = at_x * 2 + (y + dy) % 2
        swap(i, i).wait_recv()
        total = hid_send[i] + hid_recv[i]
        parts = []
        for h in range(2):
            width = total.shape[1] // 2
            grad = total[:, h * width:(h + 1) * width]
            a = stored_chip[h, 0, chip].astype(F32)
            b = stored_chip[h, 1, chip].astype(F32)
            squashed = jax.nn.sigmoid(a)
            parts.append((grad * b * squashed * (1.0 + a * (1.0 - squashed))).astype(BF16))
            parts.append((grad * a * squashed).astype(BF16))
        pre = jnp.concatenate(parts, axis=1)
        value = jnp.dot(pre, w_in_chip[...].reshape(-1, half), preferred_element_type=F32)
        if s == 1:
            ret_send[c * 2 + f] = value.astype(BF16)
            got_ret[c, f] = go(remote(
                ret_send.at[c * 2 + f], ret_sec.at[c * 2 + f], (p, second)))
        else:
            acc[c * 2 + f] = value

    got_ret = {}
    hidden((0, 0, 0))
    got_x[0, 1, 0].wait_recv()
    forward((0, 1, 0), "second")
    hidden((0, 1, 0))
    got_x[1, 0, 0].wait_recv()
    forward((1, 0, 0), "first")
    forward((1, 0, 0), "second")
    hidden((1, 0, 0))
    load_stored.wait()
    got_stored.wait_recv()
    load_in.wait()
    got_in.wait_recv()
    finish((0, 0, 0))
    got_x[0, 0, 1].wait_recv()
    hidden((0, 0, 1))
    got_x[1, 1, 0].wait_recv()
    forward((1, 1, 0), "second")
    hidden((1, 1, 0))
    finish((0, 0, 1))
    finish((0, 1, 0))
    finish((1, 0, 0))
    got_x[0, 1, 1].wait_recv()
    hidden((0, 1, 1))
    got_x[1, 0, 1].wait_recv()
    hidden((1, 0, 1))
    finish((0, 1, 1))
    finish((1, 0, 1))
    got_x[1, 1, 1].wait_recv()
    hidden((1, 1, 1))
    finish((1, 1, 0))
    finish((1, 1, 1))

    got_first = {}
    for c in (0, 1):
        got_ret[c, 1].wait_recv()
        first_send[c] = (acc[c * 2 + 1] + ret_sec[c * 2 + 1].astype(F32)).astype(BF16)
        got_first[c] = go(remote(first_send.at[c], ret_first.at[c], (p, first)))

    def summed(c):
        got_ret[c, 0].wait_recv()
        part = acc[c * 2] + ret_sec[c * 2].astype(F32)
        got_first[c].wait_recv()
        return part + ret_first[c].astype(F32)

    wide = landed.shape[2] - spare
    step = rows - wide
    z_final, z_arrival = {}, {}

    def relay(w, total):
        final[w] = (raw[w].astype(F32) + total).astype(BF16)
        index = take()
        take()
        for k in range(2):
            z_final[w, k] = pltpu.make_async_remote_copy(
                src_ref=final.at[w, pl.ds(k * step, wide)],
                dst_ref=landed.at[w, core, pl.ds(0, wide)],
                send_sem=send_sem.at[index + k], recv_sem=recv_sem.at[index + core],
                device_id=(z_to[w], base + k), device_id_type=MESH)
            z_arrival[w, k] = pltpu.make_async_remote_copy(
                src_ref=final.at[w, pl.ds(k * step, wide)],
                dst_ref=landed.at[w, k, pl.ds(0, wide)],
                send_sem=send_sem.at[index + k], recv_sem=recv_sem.at[index + k],
                device_id=(z_to[w], base + k), device_id_type=MESH)

        @pl.when(valid(z_to[w]))
        def _():
            for k in range(2):
                z_final[w, k].start()

    own_total = summed(0)
    relay(0, own_total)
    cut_send[...] = summed(1).astype(BF16)
    got_cut = go(remote(cut_send, ret_cut, (p, cut)))
    got_cut.wait_recv()
    relay(1, ret_cut[...].astype(F32))

    eye = iota((tokens, tokens), 0) == iota((tokens, tokens), 1)
    stores = []
    for w, direction in enumerate((g, 1 - g)):
        @pl.when(valid(z_from[w]))
        def _():
            z_meta[w].wait_recv()
            z_early[w].wait_recv()
            slot_row = meta[2 + w, pl.ds(direction, 1), 0:tokens]
            rank_row = unrouted(slot_row)
            slot_col = jnp.sum(jnp.where(eye, slot_row, 0.0), axis=1, keepdims=True)
            rank_col = jnp.sum(jnp.where(eye, rank_row, 0.0), axis=1, keepdims=True)
            shift = (core * (capacity - step)).astype(F32)
            column = iota((tokens, wide + spare), 1)
            late = jnp.logical_and(slot_col >= 0, column == slot_col + shift)
            soon = jnp.logical_and(rank_col >= 0, column == rank_col + float(wide))
            select = jnp.where(jnp.logical_or(late, soon), 1.0, 0.0).astype(BF16)
            for k in range(2):
                z_arrival[w, k].wait_recv()
            for h in range(2):
                out_buf[w, :, h * half:(h + 1) * half] = jnp.dot(
                    select, landed[w, h], preferred_element_type=F32).astype(BF16)

        @pl.when(jnp.logical_not(valid(z_from[w])))
        def _():
            out_buf[w] = jnp.zeros_like(out_buf[w])

        stores.append(local(out_buf.at[w], out_hbm.at[direction], 5 + w))
        stores[w].start()

    for copy in pending:
        copy.wait_send()
    for w in range(2):
        @pl.when(valid(z_to[w]))
        def _():
            z_meta[w].wait_send()
            z_early[w].wait_send()
            for k in range(2):
                z_final[w, k].wait_send()
    for store in stores:
        store.wait()


COPIES = 64


def on_device(n_pipe, grad_out, route_slot, gate_weight, stored_pre, w_in, w_out):
    _, sources, capacity, _, hidden = stored_pre.shape
    _, tokens, features = grad_out.shape
    half, rows, chips = features // 2, 2 * capacity, sources // 2
    wide = -(-capacity // 16) * 16
    spare = -(-(tokens - capacity) // 16) * 16
    stored = jnp.transpose(stored_pre[0], (2, 0, 1, 3)).reshape(2, chips, rows, hidden)
    weight_in = jnp.transpose(w_in[0], (1, 0, 2))
    hbm = pl.BlockSpec(memory_space=pl.ANY)
    vmem = pl.BlockSpec(memory_space=pltpu.VMEM)
    half_rows = (rows, half)
    return pl.pallas_call(
        functools.partial(kernel, n_pipe, capacity),
        out_shape=jax.ShapeDtypeStruct(grad_out.shape, BF16),
        in_specs=[hbm, vmem, vmem, hbm, hbm, hbm],
        out_specs=hbm,
        scratch_shapes=[
            pltpu.VMEM((2, tokens, features), BF16),
            pltpu.VMEM((2, 2, tokens, half), BF16),
            pltpu.VMEM((4, 8, 2 * tokens), F32),
            pltpu.VMEM((2, hidden, half), BF16),
            pltpu.VMEM((2, 2, hidden, half), BF16),
            pltpu.VMEM((2, 2, chips, rows, hidden), BF16),
            pltpu.VMEM((2,) + half_rows, BF16),
            pltpu.VMEM(half_rows, BF16),
            pltpu.VMEM((8,) + half_rows, BF16),
            pltpu.VMEM((8, rows, 2 * hidden), F32),
            pltpu.VMEM((8, rows, 2 * hidden), F32),
            pltpu.VMEM((4,) + half_rows, F32),
            pltpu.VMEM((4,) + half_rows, BF16),
            pltpu.VMEM((4,) + half_rows, BF16),
            pltpu.VMEM((2,) + half_rows, BF16),
            pltpu.VMEM((2,) + half_rows, BF16),
            pltpu.VMEM(half_rows, BF16),
            pltpu.VMEM(half_rows, BF16),
            pltpu.VMEM((2,) + half_rows, BF16),
            pltpu.VMEM((2, 2, spare, half), BF16),
            pltpu.VMEM((2, 2, wide + spare, half), BF16),
            pltpu.VMEM((2, tokens, features), BF16),
            pltpu.SemaphoreType.DMA((8,)),
            pltpu.SemaphoreType.DMA((COPIES,)),
            pltpu.SemaphoreType.DMA((COPIES,)),
        ],
        compiler_params=pltpu.CompilerParams(
            collective_id=0, has_side_effects=True, vmem_limit_bytes=48 * 2**20),
    )(grad_out, route_slot, gate_weight, stored, weight_in, w_out[0])


def solution(mesh):
    return jax.shard_map(
        functools.partial(on_device, mesh.shape["pipe"]),
        mesh=mesh,
        in_specs=(
            P(None, ("pipe", "expert"), None),
            P(None, ("pipe", "expert")),
            P(None, ("pipe", "expert")),
            P("pipe", None, None, None, "expert"),
            P("pipe", "expert", None, None),
            P("pipe", "expert", None),
        ),
        out_specs=P(None, ("pipe", "expert"), None),
        check_vma=False,
    )
```

time: 195 us -> 78.6 us (0.40); the launches traced: 192 us -> 78.4 us
  waiting for transfers between devices: 137 us -> 0 us
  Pallas kernels: 0 us -> 74.4 us
  starting transfers between devices: 27.7 us -> 0 us
  matrix products: 10 us -> 0 us
  other arithmetic: 8.2 us -> 0 us
  local copies, waits for them, and re-layouts: 8.54 us -> 3.91 us
    all_to_all x2 -> x0, waiting for transfers between devices: 122 us -> none  [the longest x1 63.1 us: on_device(): lax.all_to_all(partial_value, 'expert', split_axis=0, concat_axis=0, tile...]
    pallas_call x0 -> x1, Pallas kernels: none -> 74.4 us  [on_device(): pl.pallas_call(functools.partial(kernel, n_pipe, capacity), out_shape=jax...]
    ppermute x2 -> x0, waiting for transfers between devices: 15.2 us -> none  [from_behind(): lax.ppermute(value, axis, [(source, source + steps) for source in range(f...]
    all_to_all x2 -> x0, starting transfers between devices: 14 us -> none  [the longest x1 7.78 us: on_device(): lax.all_to_all(partial_value, 'expert', split_axis=0, concat_axis=0, tile...]
    ppermute x2 -> x0, starting transfers between devices: 13.7 us -> none  [from_behind(): lax.ppermute(value, axis, [(source, source + steps) for source in range(f...]
    dot_general x4 -> x0, matrix products: 10 us -> none  [the longest x1 3.82 us: expert_partial(): lax.dot_general(flat_rows, weight_out, (((1,), (1,)), ((), ())), preferre...]
    another operation x3 -> x0, local copies, waits for them, and re-layouts: 5.18 us -> none  [the longest x1 4.06 us: expert_partial(): weight_in.reshape(-1, features)]
    reduce_sum x1 -> x0, other arithmetic: 3.08 us -> none  [on_device(): jnp.sum(returned[:half_count].astype(jnp.float32), axis=0)]
  transfers between devices with their start and end apart: 4 -> 0, of which waited for: 4 -> 0; matrix products, arithmetic and copies ran while one was open for 2% -> 0% of each run, Pallas kernels for 0% -> 0%
where the time goes in v1:
time: 78.6 us; the launch traced here: 78.4 us
  Pallas kernels  74.4 us (95%)
  local copies, waits for them, and re-layouts  3.91 us (5%)
    pallas_call x1, Pallas kernels, on_device(): pl.pallas_call(functools.partial(kernel, n_pipe, capacity), out_shape=jax...  74.4 us
    unnamed x10, local copies, waits for them, and re-layouts  2.9 us

profile of v1, /device:TPU:25, one launch (start us, length us, event | category | flops | bytes accessed | tf_op | source)
XLA Modules:
  0.0 78.4 jit_solution(4345724963196153537)
XLA Ops:
  0.0 1.0 %copy.7 = bf16[2,16,40,128]{3,2,1,0:T(8,128)(2,1)S(1)} copy(bf16[2,16,40,128]{3,0,2,1:T(2,128)(2,1)} %bitcast.13) | data formatting | bytes 655360 | tf_op jit(solution)/shard_map/transpose | solution.py:354
  1.0 0.0 copy-start
  1.0 0.0 copy-start.1
  1.0 0.0 copy-start.2
  1.1 0.0 copy-start.3
  1.1 1.8 %copy.10 = bf16[1,128,2,3584]{3,1,2,0:T(8,128)(2,1)S(1)} copy(bf16[1,128,2,3584]{3,2,1,0:T(2,128)(2,1)} %param.10) | data formatting | bytes 3670016 | tf_op args[4]
  2.9 0.0 copy-done
  2.9 0.1 copy-done.1
  3.0 0.0 copy-done.2
  3.0 0.0 copy-done.3
  3.0 74.4 %shard_map.64 = bf16[2,64,3584]{2,1,0:T(8,128)(2,1)S(1)} custom-call(bf16[2,64,3584]{2,1,0:T(8,128)(2,1)S(1)} %copy-done, s32[2,64]{1,0:T(2,128)S(1)} %copy-done.2, f32[2,64]{1,0:T(2,128)S(1)} %copy-done.3, bf16[2,8,80,128]{3,2,1,0:T(8,128)(2,1)S(1)} %bitcast.11, bf16[2,128,3584]{2,1,0:T(8,128)(2,1)S(1)} %bitcast.10, bf16[128,3584]{1,0:T(8,128)(2,1)S(1)} %bitcast.12), custom_call_target="tpu_custom_call" | custom-call | tf_op jit(solution)/shard_map/pallas_call | solution.py:359
  77.5 0.9 %copy.12 = bf16[2,64,3584]{2,1,0:T(8,128)(2,1)} copy(bf16[2,64,3584]{2,1,0:T(8,128)(2,1)S(1)} %shard_map.64) | data formatting | bytes 1835008
Async XLA Ops:
  1.0 1.9 %copy-start = (bf16[2,64,3584]{2,1,0:T(8,128)(2,1)S(1)}, bf16[2,64,3584]{2,1,0:T(8,128)(2,1)}, u32[]{:S(2)}) copy-start(bf16[2,64,3584]{2,1,0:T(8,128)(2,1)} %grad_hbm.1) | copy-start | bytes 2752516
  1.0 2.0 %copy-start.1 = (bf16[1,128,3584]{2,1,0:T(8,128)(2,1)S(1)}, bf16[1,128,3584]{2,1,0:T(8,128)(2,1)}, u32[]{:S(2)}) copy-start(bf16[1,128,3584]{2,1,0:T(8,128)(2,1)} %param.11) | copy-start | bytes 2752516
  1.0 2.0 %copy-start.2 = (s32[2,64]{1,0:T(2,128)S(1)}, s32[2,64]{1,0:T(2,128)}, u32[]{:S(2)}) copy-start(s32[2,64]{1,0:T(2,128)} %slot_ref.1) | copy-start | bytes 1540
  1.1 2.0 %copy-start.3 = (f32[2,64]{1,0:T(2,128)S(1)}, f32[2,64]{1,0:T(2,128)}, u32[]{:S(2)}) copy-start(f32[2,64]{1,0:T(2,128)} %gate_ref.1) | copy-start | bytes 1540

commit v2 on v1

v2 whole, which is shorter than its diff:
```python
import functools

import jax
import jax.numpy as jnp
from jax import lax
from jax.experimental import pallas as pl
from jax.experimental.pallas import tpu as pltpu
from jax.sharding import PartitionSpec as P

MESH = pl.DeviceIdType.MESH
F32, BF16 = jnp.float32, jnp.bfloat16
BLOCKS = [(c, f, s) for c in range(2) for f in range(2) for s in range(2)]


def number(block):
    return block[0] * 4 + block[1] * 2 + block[2]


def iota(shape, dim):
    return lax.broadcasted_iota(jnp.int32, shape, dim).astype(F32)


def kernel(
    n_pipe, capacity,
    grad_hbm, slot_ref, gate_ref, stored_hbm, w_in_hbm, w_out_hbm,
    out_hbm,
    grad_chip, meta, w_out_chip, w_in_raw, w_in_chip, stored_raw, stored_chip,
    raw, cross_block, x_block, hid_send, hid_recv, acc, ret_send, ret_sec,
    first_send, ret_first, cut_send, ret_cut, final, early, place, landed, landed_place, stage,
    local_sem, send_sem, recv_sem,
):
    tokens, half = grad_chip.shape[2:]
    rows, all_tokens = 2 * capacity, 2 * tokens
    pieces = [(0, (rows // 2 + 15) // 16 * 16)]
    pieces.append((pieces[0][1], rows - pieces[0][1]))
    p, e = lax.axis_index("pipe"), lax.axis_index("expert")
    core, y, x = e % 2, (e // 2) % 2, e // 4
    g = x // 2
    sibling = e + 1 - 2 * core
    x_next = e + 4 - 8 * (x % 2)
    y_next = e + 2 - 4 * y
    cut = e + 4 * (3 - 2 * x)
    first = x_next + core * (y_next - x_next)
    second = y_next + core * (x_next - y_next)
    z_to = [p - 1 + 2 * g, p + 1 - 2 * g]
    z_from = [z_to[1], z_to[0]]
    directions = [g, 1 - g]

    def valid(rank):
        return jnp.logical_and(rank >= 0, rank < n_pipe)

    counter = [0]

    def take(count=1):
        counter[0] += count
        return counter[0] - count

    def remote(src, dst, device):
        index = take()
        return pltpu.make_async_remote_copy(
            src_ref=src, dst_ref=dst, send_sem=send_sem.at[index], recv_sem=recv_sem.at[index],
            device_id=device, device_id_type=MESH,
        )

    local_counter = [0]

    def local(src, dst):
        local_counter[0] += 1
        copy = pltpu.make_async_copy(src, dst, local_sem.at[local_counter[0] - 1])
        copy.start()
        return copy

    barrier = pltpu.get_barrier_semaphore()
    for other in (sibling, first, second, cut):
        pl.semaphore_signal(barrier, inc=1, device_id=(p, other), device_id_type=MESH)
    for rank in z_to:
        @pl.when(valid(rank))
        def _():
            pl.semaphore_signal(barrier, inc=1, device_id=(rank, e), device_id_type=MESH)

    mine = pl.multiple_of(core * half, 128)
    theirs = pl.multiple_of((1 - core) * half, 128)

    load_grad = [None, None]
    for w in (1, 0):
        load_grad[w] = local(
            grad_hbm.at[directions[w], :, pl.ds(mine, half)], grad_chip.at[w, core])

    slot = slot_ref[...].astype(F32)
    gate = gate_ref[...]
    meta[0] = jnp.zeros_like(meta[0])
    meta[0, 0:2, 0:tokens] = slot
    meta[0, 0:2, tokens:all_tokens] = slot
    meta[0, 2:4, 0:tokens] = gate
    meta[0, 2:4, tokens:all_tokens] = gate

    pl.semaphore_wait(barrier, 4 + sum(valid(rank).astype(jnp.int32) for rank in z_to))

    pending = []

    def go(copy):
        copy.start()
        pending.append(copy)
        return copy

    got_meta = go(remote(meta.at[0], meta.at[1], (p, sibling)))
    got_grad = [None, None]
    for w in (1, 0):
        got_grad[w] = go(remote(
            grad_hbm.at[directions[w], :, pl.ds(theirs, half)], grad_chip.at[w, core],
            (p, sibling)))
    load_out = local(w_out_hbm.at[0, :, pl.ds(mine, half)], w_out_chip.at[core])
    load_stored = local(stored_hbm.at[0], stored_raw.at[core])
    load_in = local(w_in_hbm.at[0, :, :, pl.ds(mine, half)], w_in_raw.at[core])
    got_out = go(remote(w_out_hbm.at[0, :, pl.ds(theirs, half)], w_out_chip.at[core], (p, sibling)))
    got_stored = go(remote(stored_hbm.at[0], stored_raw.at[core], (p, sibling)))
    got_in = go(remote(
        w_in_hbm.at[0, :, :, pl.ds(theirs, half)], w_in_raw.at[core], (p, sibling)))
    got_meta.wait_recv()

    lane = lax.broadcasted_iota(jnp.int32, (1, all_tokens), 1)
    is_own = (lane // tokens) == core
    earlier = jnp.where(
        iota((all_tokens, all_tokens), 0) < iota((all_tokens, all_tokens), 1), 1.0, 0.0
    ).astype(BF16)

    def pack(w):
        row = pl.ds(directions[w], 1)
        gate_row = pl.ds(directions[w] + 2, 1)
        chip_slot = jnp.where(is_own, meta[0, row, :], meta[1, row, :])
        chip_gate = jnp.where(is_own, meta[0, gate_row, :], meta[1, gate_row, :])
        free = jnp.broadcast_to(jnp.where(chip_slot < 0, 1.0, 0.0), (8, all_tokens))
        rank = jnp.dot(free.astype(BF16), earlier, preferred_element_type=F32)[0:1]
        position = jnp.where(
            chip_slot < 0, rank + float(rows),
            chip_slot + jnp.where(lane >= tokens, float(capacity), 0.0))
        place[w] = jnp.broadcast_to(position, place.shape[1:])
        onehot = jnp.where(iota((all_tokens, all_tokens), 0) == position, 1.0, 0.0)
        slot_gate = jnp.sum(onehot[:rows] * chip_gate, axis=1, keepdims=True)
        load_grad[w].wait()
        got_grad[w].wait_recv()
        both = jnp.concatenate([grad_chip[w, 0], grad_chip[w, 1]], axis=0)
        picked = jnp.dot(onehot.astype(BF16), both, preferred_element_type=F32)
        raw[w] = picked[:rows].astype(BF16)
        early[w] = picked[rows:].astype(BF16)
        return (slot_gate * picked[:rows]).astype(BF16)

    cross_block[...] = pack(1)
    got_x = {}
    got_x[1, 0, 0] = go(remote(cross_block, x_block.at[number((1, 0, 0))], (p, cut)))
    x_block[0] = pack(0)

    def forward(block, along):
        c, f, s = block
        target = (c, 1, s) if along == "first" else (c, f, 1)
        device = first if along == "first" else second
        got_x[target] = go(remote(
            x_block.at[number(block)], x_block.at[number(target)], (p, device)))

    forward((0, 0, 0), "first")
    forward((0, 0, 0), "second")

    z_place = [remote(place.at[w], landed_place.at[w], (z_to[w], e)) for w in range(2)]
    z_early = [
        remote(early.at[w], landed.at[w, pl.ds(rows, all_tokens - rows)], (z_to[w], e))
        for w in range(2)]
    for w in range(2):
        @pl.when(valid(z_to[w]))
        def _():
            z_place[w].start()
            z_early[w].start()

    load_out.wait()
    got_out.wait_recv()
    hid_base = take(len(BLOCKS))

    def swap(i, there):
        return pltpu.make_async_remote_copy(
            src_ref=hid_send.at[i], dst_ref=hid_recv.at[there],
            send_sem=send_sem.at[hid_base + i], recv_sem=recv_sem.at[hid_base + there],
            device_id=(p, sibling), device_id_type=MESH)

    def hidden(block):
        i = number(block)
        w_out = w_out_chip[...].reshape(-1, half)
        hid_send[i] = lax.dot_general(
            x_block[i], w_out, (((1,), (1,)), ((), ())), preferred_element_type=F32)
        pending.append(swap(i, number((block[0], block[2], block[1]))))
        pending[-1].start()

    def finish(block):
        i = number(block)
        c, f, s = block
        dx = f + core * (s - f)
        dy = s + core * (f - s)
        at_x = (x // 2) * 2 + (x % 2 + dx) % 2
        at_x = at_x + c * (3 - 2 * at_x)
        chip = at_x * 2 + (y + dy) % 2
        chip_rows = pl.ds(pl.multiple_of(chip * rows, 16), rows)
        swap(i, i).wait_recv()
        total = hid_send[i] + hid_recv[i]
        parts = []
        for h in range(2):
            width = total.shape[1] // 2
            grad = total[:, h * width:(h + 1) * width]
            a = stored_chip[h, 0, chip_rows, :].astype(F32)
            b = stored_chip[h, 1, chip_rows, :].astype(F32)
            squashed = jax.nn.sigmoid(a)
            parts.append((grad * b * squashed * (1.0 + a * (1.0 - squashed))).astype(BF16))
            parts.append((grad * a * squashed).astype(BF16))
        pre = jnp.concatenate(parts, axis=1)
        value = jnp.dot(pre, w_in_chip[...].reshape(-1, half), preferred_element_type=F32)
        if s == 1:
            ret_send[c * 2 + f] = value.astype(BF16)
        else:
            acc[c * 2 + f] = value

    def in_pieces(src, dst, other):
        return [go(remote(src.at[pl.ds(*piece)], dst.at[pl.ds(*piece)], (p, other)))
                for piece in pieces]

    got_ret, got_first = {}, {}

    def send_second(c, f):
        got_ret[c, f] = in_pieces(ret_send.at[c * 2 + f], ret_sec.at[c * 2 + f], second)

    def send_first(c):
        got_first[c] = []
        for k, (start, count) in enumerate(pieces):
            span = pl.ds(start, count)
            got_ret[c, 1][k].wait_recv()
            first_send[c, span] = (
                acc[c * 2 + 1, span] + ret_sec[c * 2 + 1, span].astype(F32)).astype(BF16)
            got_first[c].append(go(remote(
                first_send.at[c, span], ret_first.at[c, span], (p, first))))

    def summed(c, k):
        span = pl.ds(*pieces[k])
        got_ret[c, 0][k].wait_recv()
        part = acc[c * 2, span] + ret_sec[c * 2, span].astype(F32)
        got_first[c][k].wait_recv()
        return part + ret_first[c, span].astype(F32)

    def arrive(block):
        got_x[block].wait_recv()
        hidden(block)

    hidden((0, 0, 0))
    load_stored.wait()
    got_stored.wait_recv()
    load_in.wait()
    got_in.wait_recv()
    for h in range(2):
        hidden_units = stored_chip.shape[3]
        stored_chip[h] = jnp.transpose(
            stored_raw[h].reshape(-1, 2, hidden_units), (1, 0, 2))
        w_in_chip[h] = jnp.transpose(w_in_raw[h], (1, 0, 2))
    got_x[1, 0, 0].wait_recv()
    forward((1, 0, 0), "first")
    forward((1, 0, 0), "second")
    hidden((1, 0, 0))
    arrive((0, 1, 0))
    arrive((0, 0, 1))
    finish((0, 0, 0))
    finish((1, 0, 0))
    got_x[1, 1, 0].wait_recv()
    forward((1, 1, 0), "second")
    forward((0, 1, 0), "second")
    hidden((1, 1, 0))
    arrive((1, 0, 1))
    finish((1, 0, 1))
    finish((1, 1, 0))
    finish((0, 1, 0))
    arrive((1, 1, 1))
    finish((1, 1, 1))
    send_second(1, 1)
    send_second(1, 0)
    finish((0, 0, 1))
    arrive((0, 1, 1))
    finish((0, 1, 1))
    send_second(0, 1)
    send_second(0, 0)

    send_first(1)
    got_cut = []
    for k, (start, count) in enumerate(pieces):
        span = pl.ds(start, count)
        cut_send[span] = summed(1, k).astype(BF16)
        got_cut.append(go(remote(cut_send.at[span], ret_cut.at[span], (p, cut))))
    send_first(0)

    z_late = [[], []]

    def relay(w, k, total):
        span = pl.ds(*pieces[k])
        final[w, span] = (raw[w, span].astype(F32) + total).astype(BF16)
        copy = remote(final.at[w, span], landed.at[w, span], (z_to[w], e))
        z_late[w].append(copy)

        @pl.when(valid(z_to[w]))
        def _():
            copy.start()

    for k in range(len(pieces)):
        got_cut[k].wait_recv()
        relay(1, k, ret_cut[pl.ds(*pieces[k])].astype(F32))
    for k in range(len(pieces)):
        relay(0, k, summed(0, k))

    eye = iota((all_tokens, all_tokens), 0) == iota((all_tokens, all_tokens), 1)
    stores = []
    for w in (1, 0):
        @pl.when(valid(z_from[w]))
        def _():
            z_place[w].wait_recv()
            z_early[w].wait_recv()
            position = jnp.sum(
                jnp.where(eye, landed_place[w, 0:1, :], 0.0), axis=1, keepdims=True)
            select = jnp.where(
                iota((all_tokens, all_tokens), 1) == position, 1.0, 0.0).astype(BF16)
            for copy in z_late[w]:
                copy.wait_recv()
            value = jnp.dot(select, landed[w], preferred_element_type=F32).astype(BF16)
            stage[w, 0] = value[:tokens]
            stage[w, 1] = value[tokens:]

        @pl.when(jnp.logical_not(valid(z_from[w])))
        def _():
            stage[w] = jnp.zeros_like(stage[w])

        target = out_hbm.at[directions[w], :, pl.ds(mine, half)]
        stores.append(go(remote(stage.at[w, 1 - core], target, (p, sibling))).wait_recv)
        stores.append(local(stage.at[w, core], target).wait)

    for wait in stores:
        wait()
    for copy in pending:
        copy.wait_send()
    for w in range(2):
        @pl.when(valid(z_to[w]))
        def _():
            for copy in [z_place[w], z_early[w]] + z_late[w]:
                copy.wait_send()


COPIES = 64


def on_device(n_pipe, grad_out, route_slot, gate_weight, stored_pre, w_in, w_out):
    _, sources, capacity, _, hidden = stored_pre.shape
    _, tokens, features = grad_out.shape
    half, rows, chips = features // 2, 2 * capacity, sources // 2
    hbm = pl.BlockSpec(memory_space=pltpu.HBM)
    vmem = pl.BlockSpec(memory_space=pltpu.VMEM)
    half_rows = (rows, half)
    return pl.pallas_call(
        functools.partial(kernel, n_pipe, capacity),
        out_shape=jax.ShapeDtypeStruct(grad_out.shape, BF16),
        in_specs=[hbm, vmem, vmem, hbm, hbm, hbm],
        out_specs=hbm,
        scratch_shapes=[
            pltpu.VMEM((2, 2, tokens, half), BF16),
            pltpu.VMEM((2, 8, 2 * tokens), F32),
            pltpu.VMEM((2, hidden, half), BF16),
            pltpu.VMEM((2, hidden, 2, half), BF16),
            pltpu.VMEM((2, 2, hidden, half), BF16),
            pltpu.VMEM((2, sources, capacity, 2, hidden), BF16),
            pltpu.VMEM((2, 2, sources * capacity, hidden), BF16),
            pltpu.VMEM((2,) + half_rows, BF16),
            pltpu.VMEM(half_rows, BF16),
            pltpu.VMEM((8,) + half_rows, BF16),
            pltpu.VMEM((8, rows, 2 * hidden), F32),
            pltpu.VMEM((8, rows, 2 * hidden), F32),
            pltpu.VMEM((4,) + half_rows, F32),
            pltpu.VMEM((4,) + half_rows, BF16),
            pltpu.VMEM((4,) + half_rows, BF16),
            pltpu.VMEM((2,) + half_rows, BF16),
            pltpu.VMEM((2,) + half_rows, BF16),
            pltpu.VMEM(half_rows, BF16),
            pltpu.VMEM(half_rows, BF16),
            pltpu.VMEM((2,) + half_rows, BF16),
            pltpu.VMEM((2, 2 * tokens - rows, half), BF16),
            pltpu.VMEM((2, 8, 2 * tokens), F32),
            pltpu.VMEM((2, 2 * tokens, half), BF16),
            pltpu.VMEM((2, 8, 2 * tokens), F32),
            pltpu.VMEM((2, 2, tokens, half), BF16),
            pltpu.SemaphoreType.DMA((8,)),
            pltpu.SemaphoreType.DMA((COPIES,)),
            pltpu.SemaphoreType.DMA((COPIES,)),
        ],
        compiler_params=pltpu.CompilerParams(
            collective_id=0, has_side_effects=True, vmem_limit_bytes=62 * 2**20),
    )(grad_out, route_slot, gate_weight, stored_pre, w_in, w_out)


def solution(mesh):
    return jax.shard_map(
        functools.partial(on_device, mesh.shape["pipe"]),
        mesh=mesh,
        in_specs=(
            P(None, ("pipe", "expert"), None),
            P(None, ("pipe", "expert")),
            P(None, ("pipe", "expert")),
            P("pipe", None, None, None, "expert"),
            P("pipe", "expert", None, None),
            P("pipe", "expert", None),
        ),
        out_specs=P(None, ("pipe", "expert"), None),
        check_vma=False,
    )
```

time: 78.6 us -> 70.1 us (0.89)
  Pallas kernels: 74.4 us -> 67 us
  local copies, waits for them, and re-layouts: 3.91 us -> 2.16 us
    pallas_call x1, Pallas kernels: 74.4 us -> 67 us  [on_device(): pl.pallas_call(functools.partial(kernel, n_pipe, capacity), out_shape=jax...]
    transpose x1 -> x0, local copies, waits for them, and re-layouts: 1.02 us -> none  [on_device(): jnp.transpose(stored_pre[0], (2, 0, 1, 3)).reshape(2, chips, rows, hidden)]
    unnamed x10 -> x1, local copies, waits for them, and re-layouts: 2.9 us -> 2.16 us
where the time goes in v2:
time: 70.1 us; the launch traced here: 69.2 us
  Pallas kernels  67 us (96%)
  local copies, waits for them, and re-layouts  2.16 us (3%)
    pallas_call x1, Pallas kernels, on_device(): pl.pallas_call(functools.partial(kernel, n_pipe, capacity), out_shape=jax...  67 us
    unnamed x1, local copies, waits for them, and re-layouts  2.16 us

profile of v2, /device:TPU:25, one launch (start us, length us, event | category | flops | bytes accessed | tf_op | source)
XLA Modules:
  0.0 69.2 jit_solution(625564600276249959)
XLA Ops:
  0.0 67.0 %shard_map.64 = bf16[2,64,3584]{2,1,0:T(8,128)(2,1)} custom-call(bf16[2,64,3584]{2,1,0:T(8,128)(2,1)} %grad_hbm.1, s32[2,64]{1,0:T(2,128)} %slot_ref.1, f32[2,64]{1,0:T(2,128)} %gate_ref.1, bf16[1,16,40,2,128]{4,3,2,1,0:T(2,128)(2,1)} %stored_hbm.1, bf16[1,128,2,3584]{3,2,1,0:T(2,128)(2,1)} %w_in_hbm.1, bf16[1,128,3584]{2,1,0:T(8,128)(2,1)} %w_out_hbm.1), custom_call_target="tpu_custom_call" | custom-call | tf_op jit(solution)/shard_map/pallas_call | solution.py:356
  67.0 2.2 %copy.8 = bf16[2,64,3584]{2,1,0:T(8,128)(2,1)} copy(bf16[2,64,3584]{2,1,0:T(8,128)(2,1)} %shard_map.64) | data formatting | bytes 1835008

commit v3 on v2

--- a/solution.py
+++ b/solution.py
@@ -12,6 +12,14 @@
 BLOCKS = [(c, f, s) for c in range(2) for f in range(2) for s in range(2)]
 
 
+OUT_ROWS, BACK_ROWS = 16, 16
+COPIES = 200
+
+
+def row_pieces(rows, most):
+    return [(start, min(most, rows - start)) for start in range(0, rows, most)]
+
+
 def number(block):
     return block[0] * 4 + block[1] * 2 + block[2]
 
@@ -25,14 +33,13 @@
     grad_hbm, slot_ref, gate_ref, stored_hbm, w_in_hbm, w_out_hbm,
     out_hbm,
     grad_chip, meta, w_out_chip, w_in_raw, w_in_chip, stored_raw, stored_chip,
-    raw, cross_block, x_block, hid_send, hid_recv, acc, ret_send, ret_sec,
-    first_send, ret_first, cut_send, ret_cut, final, early, place, landed, landed_place, stage,
+    cross_block, x_block, cross_gate, x_gate, hid_send, hid_recv, acc, ret_send, ret_sec,
+    first_send, ret_first, final, ret_cut, early, place, landed, landed_place, stage,
     local_sem, send_sem, recv_sem,
 ):
     tokens, half = grad_chip.shape[2:]
     rows, all_tokens = 2 * capacity, 2 * tokens
-    pieces = [(0, (rows // 2 + 15) // 16 * 16)]
-    pieces.append((pieces[0][1], rows - pieces[0][1]))
+    out_pieces, pieces = row_pieces(rows, OUT_ROWS), row_pieces(rows, BACK_ROWS)
     p, e = lax.axis_index("pipe"), lax.axis_index("expert")
     core, y, x = e % 2, (e // 2) % 2, e // 4
     g = x // 2
@@ -70,6 +77,14 @@
         copy.start()
         return copy
 
+    def far(rank):
+        ring = n_pipe // 2
+        return jnp.logical_and(valid(rank), rank // ring != p // ring)
+
+    is_far = [far(rank).astype(jnp.int32) for rank in z_to]
+    late_to = [e + flag * (y_next - e) for flag in is_far]
+    turn_first, turn_second = is_far[0] * core, is_far[0] * (1 - core)
+
     barrier = pltpu.get_barrier_semaphore()
     for other in (sibling, first, second, cut):
         pl.semaphore_signal(barrier, inc=1, device_id=(p, other), device_id_type=MESH)
@@ -77,6 +92,10 @@
         @pl.when(valid(rank))
         def _():
             pl.semaphore_signal(barrier, inc=1, device_id=(rank, e), device_id_type=MESH)
+
+        @pl.when(far(rank))
+        def _():
+            pl.semaphore_signal(barrier, inc=1, device_id=(rank, y_next), device_id_type=MESH)
 
     mine = pl.multiple_of(core * half, 128)
     theirs = pl.multiple_of((1 - core) * half, 128)
@@ -94,7 +113,8 @@
     meta[0, 2:4, 0:tokens] = gate
     meta[0, 2:4, tokens:all_tokens] = gate
 
-    pl.semaphore_wait(barrier, 4 + sum(valid(rank).astype(jnp.int32) for rank in z_to))
+    pl.semaphore_wait(
+        barrier, 4 + sum(valid(rank).astype(jnp.int32) for rank in z_to) + sum(is_far))
 
     pending = []
 
@@ -102,6 +122,10 @@
         copy.start()
         pending.append(copy)
         return copy
+
+    def in_pieces(spans, src, dst, other):
+        return [go(remote(src.at[pl.ds(*span)], dst.at[pl.ds(*span)], (p, other)))
+                for span in spans]
 
     got_meta = go(remote(meta.at[0], meta.at[1], (p, sibling)))
     got_grad = [None, None]
@@ -123,6 +147,8 @@
     earlier = jnp.where(
         iota((all_tokens, all_tokens), 0) < iota((all_tokens, all_tokens), 1), 1.0, 0.0
     ).astype(BF16)
+
+    slot_eye = iota((rows, all_tokens), 0) == iota((rows, all_tokens), 1)
 
     def pack(w):
         row = pl.ds(directions[w], 1)
@@ -141,24 +167,39 @@
         got_grad[w].wait_recv()
         both = jnp.concatenate([grad_chip[w, 0], grad_chip[w, 1]], axis=0)
         picked = jnp.dot(onehot.astype(BF16), both, preferred_element_type=F32)
-        raw[w] = picked[:rows].astype(BF16)
         early[w] = picked[rows:].astype(BF16)
-        return (slot_gate * picked[:rows]).astype(BF16)
-
-    cross_block[...] = pack(1)
+        gates = jnp.sum(jnp.where(slot_eye, slot_gate, 0.0), axis=0, keepdims=True)
+        return picked[:rows].astype(BF16), jnp.broadcast_to(gates, cross_gate.shape)
+
+    cross_block[...], cross_gate[...] = pack(1)
     got_x = {}
-    got_x[1, 0, 0] = go(remote(cross_block, x_block.at[number((1, 0, 0))], (p, cut)))
-    x_block[0] = pack(0)
-
-    def forward(block, along):
+    got_x[1, 0, 0] = in_pieces(out_pieces, cross_block, x_block.at[number((1, 0, 0))], cut)
+    got_gate = {(1, 0, 0): go(remote(cross_gate, x_gate.at[number((1, 0, 0))], (p, cut)))}
+    x_block[0], x_gate[0] = pack(0)
+
+    def forward(block, *axes):
         c, f, s = block
-        target = (c, 1, s) if along == "first" else (c, f, 1)
-        device = first if along == "first" else second
-        got_x[target] = go(remote(
-            x_block.at[number(block)], x_block.at[number(target)], (p, device)))
-
-    forward((0, 0, 0), "first")
-    forward((0, 0, 0), "second")
+        targets = {"first": (c, 1, s), "second": (c, f, 1)}
+        for axis in axes:
+            got_x[targets[axis]] = []
+        for k, (start, count) in enumerate(out_pieces):
+            span = pl.ds(start, count)
+            if block in got_x and block not in arrived:
+                got_x[block][k].wait_recv()
+            for axis in axes:
+                got_x[targets[axis]].append(go(remote(
+                    x_block.at[number(block), span], x_block.at[number(targets[axis]), span],
+                    (p, first if axis == "first" else second))))
+        if block in got_gate and block not in arrived:
+            got_gate[block].wait_recv()
+        for axis in axes:
+            got_gate[targets[axis]] = go(remote(
+                x_gate.at[number(block)], x_gate.at[number(targets[axis])],
+                (p, first if axis == "first" else second)))
+        arrived.add(block)
+
+    arrived = set()
+    forward((0, 0, 0), "first", "second")
 
     z_place = [remote(place.at[w], landed_place.at[w], (z_to[w], e)) for w in range(2)]
     z_early = [
@@ -198,7 +239,8 @@
         chip = at_x * 2 + (y + dy) % 2
         chip_rows = pl.ds(pl.multiple_of(chip * rows, 16), rows)
         swap(i, i).wait_recv()
-        total = hid_send[i] + hid_recv[i]
+        slot_gate = jnp.sum(jnp.where(slot_eye, x_gate[i, 0:1, :], 0.0), axis=1, keepdims=True)
+        total = (hid_send[i] + hid_recv[i]) * slot_gate
         parts = []
         for h in range(2):
             width = total.shape[1] // 2
@@ -210,19 +252,18 @@
             parts.append((grad * a * squashed).astype(BF16))
         pre = jnp.concatenate(parts, axis=1)
         value = jnp.dot(pre, w_in_chip[...].reshape(-1, half), preferred_element_type=F32)
-        if s == 1:
-            ret_send[c * 2 + f] = value.astype(BF16)
-        else:
-            acc[c * 2 + f] = value
-
-    def in_pieces(src, dst, other):
-        return [go(remote(src.at[pl.ds(*piece)], dst.at[pl.ds(*piece)], (p, other)))
-                for piece in pieces]
+        acc[i] = value
+
+    def block_of(c, f, s):
+        flip = lambda bit, turn: 1 - turn if bit else turn
+        return c * 4 + flip(f, turn_first) * 2 + flip(s, turn_second)
 
     got_ret, got_first = {}, {}
 
     def send_second(c, f):
-        got_ret[c, f] = in_pieces(ret_send.at[c * 2 + f], ret_sec.at[c * 2 + f], second)
+        ret_send[c * 2 + f] = acc[block_of(c, f, 1)].astype(BF16)
+        got_ret[c, f] = in_pieces(
+            pieces, ret_send.at[c * 2 + f], ret_sec.at[c * 2 + f], second)
 
     def send_first(c):
         got_first[c] = []
@@ -230,19 +271,26 @@
             span = pl.ds(start, count)
             got_ret[c, 1][k].wait_recv()
             first_send[c, span] = (
-                acc[c * 2 + 1, span] + ret_sec[c * 2 + 1, span].astype(F32)).astype(BF16)
+                acc[block_of(c, 1, 0), span] + ret_sec[c * 2 + 1, span].astype(F32)).astype(BF16)
             got_first[c].append(go(remote(
                 first_send.at[c, span], ret_first.at[c, span], (p, first))))
 
     def summed(c, k):
         span = pl.ds(*pieces[k])
         got_ret[c, 0][k].wait_recv()
-        part = acc[c * 2, span] + ret_sec[c * 2, span].astype(F32)
+        i = block_of(c, 0, 0)
+        part = acc[i, span] + ret_sec[c * 2, span].astype(F32)
         got_first[c][k].wait_recv()
-        return part + ret_first[c, span].astype(F32)
+        total = part + ret_first[c, span].astype(F32)
+        final[c, span] = (x_block[i, span].astype(F32) + total).astype(BF16)
+        return final.at[c, span]
 
     def arrive(block):
-        got_x[block].wait_recv()
+        if block not in arrived:
+            for copy in got_x[block]:
+                copy.wait_recv()
+            got_gate[block].wait_recv()
+            arrived.add(block)
         hidden(block)
 
     hidden((0, 0, 0))
@@ -255,15 +303,12 @@
         stored_chip[h] = jnp.transpose(
             stored_raw[h].reshape(-1, 2, hidden_units), (1, 0, 2))
         w_in_chip[h] = jnp.transpose(w_in_raw[h], (1, 0, 2))
-    got_x[1, 0, 0].wait_recv()
-    forward((1, 0, 0), "first")
-    forward((1, 0, 0), "second")
+    forward((1, 0, 0), "first", "second")
     hidden((1, 0, 0))
     arrive((0, 1, 0))
     arrive((0, 0, 1))
     finish((0, 0, 0))
     finish((1, 0, 0))
-    got_x[1, 1, 0].wait_recv()
     forward((1, 1, 0), "second")
     forward((0, 1, 0), "second")
     hidden((1, 1, 0))
@@ -284,17 +329,13 @@
     send_first(1)
     got_cut = []
     for k, (start, count) in enumerate(pieces):
-        span = pl.ds(start, count)
-        cut_send[span] = summed(1, k).astype(BF16)
-        got_cut.append(go(remote(cut_send.at[span], ret_cut.at[span], (p, cut))))
+        got_cut.append(go(remote(summed(1, k), ret_cut.at[pl.ds(start, count)], (p, cut))))
     send_first(0)
 
     z_late = [[], []]
 
-    def relay(w, k, total):
-        span = pl.ds(*pieces[k])
-        final[w, span] = (raw[w, span].astype(F32) + total).astype(BF16)
-        copy = remote(final.at[w, span], landed.at[w, span], (z_to[w], e))
+    def relay(w, k, rows_ref):
+        copy = remote(rows_ref, landed.at[w, pl.ds(*pieces[k])], (z_to[w], late_to[w]))
         z_late[w].append(copy)
 
         @pl.when(valid(z_to[w]))
@@ -303,7 +344,7 @@
 
     for k in range(len(pieces)):
         got_cut[k].wait_recv()
-        relay(1, k, ret_cut[pl.ds(*pieces[k])].astype(F32))
+        relay(1, k, ret_cut.at[pl.ds(*pieces[k])])
     for k in range(len(pieces)):
         relay(0, k, summed(0, k))
 
@@ -341,9 +382,6 @@
         def _():
             for copy in [z_place[w], z_early[w]] + z_late[w]:
                 copy.wait_send()
-
-
-COPIES = 64
 
 
 def on_device(n_pipe, grad_out, route_slot, gate_weight, stored_pre, w_in, w_out):
@@ -366,19 +404,19 @@
             pltpu.VMEM((2, 2, hidden, half), BF16),
             pltpu.VMEM((2, sources, capacity, 2, hidden), BF16),
             pltpu.VMEM((2, 2, sources * capacity, hidden), BF16),
-            pltpu.VMEM((2,) + half_rows, BF16),
             pltpu.VMEM(half_rows, BF16),
             pltpu.VMEM((8,) + half_rows, BF16),
+            pltpu.VMEM((8, 2 * tokens), F32),
+            pltpu.VMEM((8, 8, 2 * tokens), F32),
             pltpu.VMEM((8, rows, 2 * hidden), F32),
             pltpu.VMEM((8, rows, 2 * hidden), F32),
-            pltpu.VMEM((4,) + half_rows, F32),
+            pltpu.VMEM((8,) + half_rows, F32),
             pltpu.VMEM((4,) + half_rows, BF16),
             pltpu.VMEM((4,) + half_rows, BF16),
             pltpu.VMEM((2,) + half_rows, BF16),
             pltpu.VMEM((2,) + half_rows, BF16),
+            pltpu.VMEM((2,) + half_rows, BF16),
             pltpu.VMEM(half_rows, BF16),
-            pltpu.VMEM(half_rows, BF16),
-            pltpu.VMEM((2,) + half_rows, BF16),
             pltpu.VMEM((2, 2 * tokens - rows, half), BF16),
             pltpu.VMEM((2, 8, 2 * tokens), F32),
             pltpu.VMEM((2, 2 * tokens, half), BF16),

time: 70.1 us -> 66.1 us (0.943)
  Pallas kernels: 67 us -> 63.4 us
    pallas_call x1, Pallas kernels: 67 us -> 63.4 us  [on_device(): pl.pallas_call(functools.partial(kernel, n_pipe, capacity), out_shape=jax...]
where the time goes in v3:
time: 66.1 us; the launch traced here: 65.6 us
  Pallas kernels  63.4 us (96%)
  local copies, waits for them, and re-layouts  2.16 us (3%)
    pallas_call x1, Pallas kernels, on_device(): pl.pallas_call(functools.partial(kernel, n_pipe, capacity), out_shape=jax...  63.4 us
    unnamed x1, local copies, waits for them, and re-layouts  2.16 us

profile of v3, /device:TPU:25, one launch (start us, length us, event | category | flops | bytes accessed | tf_op | source)
XLA Modules:
  0.0 65.6 jit_solution(9031387806554579645)
XLA Ops:
  0.0 63.4 %shard_map.64 = bf16[2,64,3584]{2,1,0:T(8,128)(2,1)} custom-call(bf16[2,64,3584]{2,1,0:T(8,128)(2,1)} %grad_hbm.1, s32[2,64]{1,0:T(2,128)} %slot_ref.1, f32[2,64]{1,0:T(2,128)} %gate_ref.1, bf16[1,16,40,2,128]{4,3,2,1,0:T(2,128)(2,1)} %stored_hbm.1, bf16[1,128,2,3584]{3,2,1,0:T(2,128)(2,1)} %w_in_hbm.1, bf16[1,128,3584]{2,1,0:T(8,128)(2,1)} %w_out_hbm.1), custom_call_target="tpu_custom_call" | custom-call | tf_op jit(solution)/shard_map/pallas_call | solution.py:394
  63.4 2.2 %copy.8 = bf16[2,64,3584]{2,1,0:T(8,128)(2,1)} copy(bf16[2,64,3584]{2,1,0:T(8,128)(2,1)} %shard_map.64) | data formatting | bytes 1835008

commit v4 on v3

--- a/solution.py
+++ b/solution.py
@@ -101,7 +101,7 @@
     theirs = pl.multiple_of((1 - core) * half, 128)
 
     load_grad = [None, None]
-    for w in (1, 0):
+    for w in (0, 1):
         load_grad[w] = local(
             grad_hbm.at[directions[w], :, pl.ds(mine, half)], grad_chip.at[w, core])
 
@@ -129,17 +129,10 @@
 
     got_meta = go(remote(meta.at[0], meta.at[1], (p, sibling)))
     got_grad = [None, None]
-    for w in (1, 0):
+    for w in (0, 1):
         got_grad[w] = go(remote(
             grad_hbm.at[directions[w], :, pl.ds(theirs, half)], grad_chip.at[w, core],
             (p, sibling)))
-    load_out = local(w_out_hbm.at[0, :, pl.ds(mine, half)], w_out_chip.at[core])
-    load_stored = local(stored_hbm.at[0], stored_raw.at[core])
-    load_in = local(w_in_hbm.at[0, :, :, pl.ds(mine, half)], w_in_raw.at[core])
-    got_out = go(remote(w_out_hbm.at[0, :, pl.ds(theirs, half)], w_out_chip.at[core], (p, sibling)))
-    got_stored = go(remote(stored_hbm.at[0], stored_raw.at[core], (p, sibling)))
-    got_in = go(remote(
-        w_in_hbm.at[0, :, :, pl.ds(theirs, half)], w_in_raw.at[core], (p, sibling)))
     got_meta.wait_recv()
 
     lane = lax.broadcasted_iota(jnp.int32, (1, all_tokens), 1)
@@ -171,11 +164,7 @@
         gates = jnp.sum(jnp.where(slot_eye, slot_gate, 0.0), axis=0, keepdims=True)
         return picked[:rows].astype(BF16), jnp.broadcast_to(gates, cross_gate.shape)
 
-    cross_block[...], cross_gate[...] = pack(1)
-    got_x = {}
-    got_x[1, 0, 0] = in_pieces(out_pieces, cross_block, x_block.at[number((1, 0, 0))], cut)
-    got_gate = {(1, 0, 0): go(remote(cross_gate, x_gate.at[number((1, 0, 0))], (p, cut)))}
-    x_block[0], x_gate[0] = pack(0)
+    got_x, got_gate, arrived = {}, {}, set()
 
     def forward(block, *axes):
         c, f, s = block
@@ -198,8 +187,19 @@
                 (p, first if axis == "first" else second)))
         arrived.add(block)
 
-    arrived = set()
+    x_block[0], x_gate[0] = pack(0)
     forward((0, 0, 0), "first", "second")
+    cross_block[...], cross_gate[...] = pack(1)
+    got_x[1, 0, 0] = in_pieces(out_pieces, cross_block, x_block.at[number((1, 0, 0))], cut)
+    got_gate[1, 0, 0] = go(remote(cross_gate, x_gate.at[number((1, 0, 0))], (p, cut)))
+
+    load_out = local(w_out_hbm.at[0, :, pl.ds(mine, half)], w_out_chip.at[core])
+    load_stored = local(stored_hbm.at[0], stored_raw.at[core])
+    load_in = local(w_in_hbm.at[0, :, :, pl.ds(mine, half)], w_in_raw.at[core])
+    got_out = go(remote(w_out_hbm.at[0, :, pl.ds(theirs, half)], w_out_chip.at[core], (p, sibling)))
+    got_stored = go(remote(stored_hbm.at[0], stored_raw.at[core], (p, sibling)))
+    got_in = go(remote(
+        w_in_hbm.at[0, :, :, pl.ds(theirs, half)], w_in_raw.at[core], (p, sibling)))
 
     z_place = [remote(place.at[w], landed_place.at[w], (z_to[w], e)) for w in range(2)]
     z_early = [

time: 66.1 us -> 66 us (level)
  no operation moved by 1% of the time
where the time goes in v4:
time: 66 us; the launch traced here: 65.1 us
  Pallas kernels  62.9 us (95%)
  local copies, waits for them, and re-layouts  2.16 us (3%)
    pallas_call x1, Pallas kernels, on_device(): pl.pallas_call(functools.partial(kernel, n_pipe, capacity), out_shape=jax...  62.9 us
    unnamed x1, local copies, waits for them, and re-layouts  2.16 us

profile of v4, /device:TPU:25, one launch (start us, length us, event | category | flops | bytes accessed | tf_op | source)
XLA Modules:
  0.0 65.1 jit_solution(11553111903133979466)
XLA Ops:
  0.0 62.9 %shard_map.64 = bf16[2,64,3584]{2,1,0:T(8,128)(2,1)} custom-call(bf16[2,64,3584]{2,1,0:T(8,128)(2,1)} %grad_hbm.1, s32[2,64]{1,0:T(2,128)} %slot_ref.1, f32[2,64]{1,0:T(2,128)} %gate_ref.1, bf16[1,16,40,2,128]{4,3,2,1,0:T(2,128)(2,1)} %stored_hbm.1, bf16[1,128,2,3584]{3,2,1,0:T(2,128)(2,1)} %w_in_hbm.1, bf16[1,128,3584]{2,1,0:T(8,128)(2,1)} %w_out_hbm.1), custom_call_target="tpu_custom_call" | custom-call | tf_op jit(solution)/shard_map/pallas_call | solution.py:394
  62.9 2.2 %copy.8 = bf16[2,64,3584]{2,1,0:T(8,128)(2,1)} copy(bf16[2,64,3584]{2,1,0:T(8,128)(2,1)} %shard_map.64) | data formatting | bytes 1835008

commit v5 on v4

--- a/solution.py
+++ b/solution.py
@@ -393,9 +393,9 @@
     half_rows = (rows, half)
     return pl.pallas_call(
         functools.partial(kernel, n_pipe, capacity),
-        out_shape=jax.ShapeDtypeStruct(grad_out.shape, BF16),
+        out_shape=pltpu.VMEM(grad_out.shape, BF16),
         in_specs=[hbm, vmem, vmem, hbm, hbm, hbm],
-        out_specs=hbm,
+        out_specs=vmem,
         scratch_shapes=[
             pltpu.VMEM((2, 2, tokens, half), BF16),
             pltpu.VMEM((2, 8, 2 * tokens), F32),
@@ -427,7 +427,7 @@
             pltpu.SemaphoreType.DMA((COPIES,)),
         ],
         compiler_params=pltpu.CompilerParams(
-            collective_id=0, has_side_effects=True, vmem_limit_bytes=62 * 2**20),
+            collective_id=0, has_side_effects=True, vmem_limit_bytes=56 * 2**20),
     )(grad_out, route_slot, gate_weight, stored_pre, w_in, w_out)
 
 

time: 66 us -> 64.6 us (0.979)
  local copies, waits for them, and re-layouts: 2.16 us -> 0.93 us
    unnamed x1, local copies, waits for them, and re-layouts: 2.16 us -> 0.93 us
where the time goes in v5:
time: 64.6 us; the launch traced here: 63.7 us
  Pallas kernels  62.8 us (97%)
  local copies, waits for them, and re-layouts  0.93 us (1%)
    pallas_call x1, Pallas kernels, on_device(): pl.pallas_call(functools.partial(kernel, n_pipe, capacity), out_shape=plt...  62.8 us

profile of v5, /device:TPU:25, one launch (start us, length us, event | category | flops | bytes accessed | tf_op | source)
XLA Modules:
  0.0 63.7 jit_solution(11759647870351716098)
XLA Ops:
  0.0 62.8 %shard_map.64 = bf16[2,64,3584]{2,1,0:T(8,128)(2,1)S(1)} custom-call(bf16[2,64,3584]{2,1,0:T(8,128)(2,1)} %grad_hbm.1, s32[2,64]{1,0:T(2,128)} %slot_ref.1, f32[2,64]{1,0:T(2,128)} %gate_ref.1, bf16[1,16,40,2,128]{4,3,2,1,0:T(2,128)(2,1)} %stored_hbm.1, bf16[1,128,2,3584]{3,2,1,0:T(2,128)(2,1)} %w_in_hbm.1, bf16[1,128,3584]{2,1,0:T(8,128)(2,1)} %w_out_hbm.1), custom_call_target="tpu_custom_call" | custom-call | tf_op jit(solution)/shard_map/pallas_call | solution.py:394
  62.8 0.9 %copy.8 = bf16[2,64,3584]{2,1,0:T(8,128)(2,1)} copy(bf16[2,64,3584]{2,1,0:T(8,128)(2,1)S(1)} %shard_map.64) | data formatting | bytes 1835008

commit v6 on v5

--- a/solution.py
+++ b/solution.py
@@ -348,30 +348,35 @@
     for k in range(len(pieces)):
         relay(0, k, summed(0, k))
 
-    eye = iota((all_tokens, all_tokens), 0) == iota((all_tokens, all_tokens), 1)
     stores = []
     for w in (1, 0):
-        @pl.when(valid(z_from[w]))
-        def _():
-            z_place[w].wait_recv()
-            z_early[w].wait_recv()
-            position = jnp.sum(
-                jnp.where(eye, landed_place[w, 0:1, :], 0.0), axis=1, keepdims=True)
-            select = jnp.where(
-                iota((all_tokens, all_tokens), 1) == position, 1.0, 0.0).astype(BF16)
-            for copy in z_late[w]:
-                copy.wait_recv()
-            value = jnp.dot(select, landed[w], preferred_element_type=F32).astype(BF16)
-            stage[w, 0] = value[:tokens]
-            stage[w, 1] = value[tokens:]
-
-        @pl.when(jnp.logical_not(valid(z_from[w])))
-        def _():
-            stage[w] = jnp.zeros_like(stage[w])
-
         target = out_hbm.at[directions[w], :, pl.ds(mine, half)]
-        stores.append(go(remote(stage.at[w, 1 - core], target, (p, sibling))).wait_recv)
-        stores.append(local(stage.at[w, core], target).wait)
+        for owner in (1 - core, core):
+            @pl.when(valid(z_from[w]))
+            def _():
+                if owner is not core:
+                    z_place[w].wait_recv()
+                    z_early[w].wait_recv()
+                shape = (tokens, all_tokens)
+                token = iota(shape, 0) + (owner * tokens).astype(F32)
+                position = jnp.sum(
+                    jnp.where(token == iota(shape, 1), landed_place[w, 0:1, :], 0.0),
+                    axis=1, keepdims=True)
+                select = jnp.where(iota(shape, 1) == position, 1.0, 0.0).astype(BF16)
+                if owner is not core:
+                    for copy in z_late[w]:
+                        copy.wait_recv()
+                stage[w, owner] = jnp.dot(
+                    select, landed[w], preferred_element_type=F32).astype(BF16)
+
+            @pl.when(jnp.logical_not(valid(z_from[w])))
+            def _():
+                stage[w, owner] = jnp.zeros(stage.shape[2:], BF16)
+
+            if owner is core:
+                stores.append(local(stage.at[w, owner], target).wait)
+            else:
+                stores.append(go(remote(stage.at[w, owner], target, (p, sibling))).wait_recv)
 
     for wait in stores:
         wait()

time: 64.6 us -> 64.5 us (level)
  no operation moved by 1% of the time
where the time goes in v6:
time: 64.5 us; the launch traced here: 63.9 us
  Pallas kernels  62.9 us (98%)
  local copies, waits for them, and re-layouts  0.93 us (1%)
    pallas_call x1, Pallas kernels, on_device(): pl.pallas_call(functools.partial(kernel, n_pipe, capacity), out_shape=plt...  62.9 us

profile of v6, /device:TPU:25, one launch (start us, length us, event | category | flops | bytes accessed | tf_op | source)
XLA Modules:
  0.0 63.9 jit_solution(7277300602699975119)
XLA Ops:
  0.0 62.9 %shard_map.64 = bf16[2,64,3584]{2,1,0:T(8,128)(2,1)S(1)} custom-call(bf16[2,64,3584]{2,1,0:T(8,128)(2,1)} %grad_hbm.1, s32[2,64]{1,0:T(2,128)} %slot_ref.1, f32[2,64]{1,0:T(2,128)} %gate_ref.1, bf16[1,16,40,2,128]{4,3,2,1,0:T(2,128)(2,1)} %stored_hbm.1, bf16[1,128,2,3584]{3,2,1,0:T(2,128)(2,1)} %w_in_hbm.1, bf16[1,128,3584]{2,1,0:T(8,128)(2,1)} %w_out_hbm.1), custom_call_target="tpu_custom_call" | custom-call | tf_op jit(solution)/shard_map/pallas_call | solution.py:399
  62.9 0.9 %copy.8 = bf16[2,64,3584]{2,1,0:T(8,128)(2,1)} copy(bf16[2,64,3584]{2,1,0:T(8,128)(2,1)S(1)} %shard_map.64) | data formatting | bytes 1835008
